TPU v7x, 128 devices: a whole 4x4x4 slice. The times are simulated.
128 devices in a mesh: row: 8 (over z, core), col: 16 (over x, y).
Axes of the slice: x: 4, y: 4, z: 4, core: 2. Of those that a mesh axis runs over, the one named last changes fastest.
Arguments:
- embeddings: float32 [32768, 768], P(('row', 'col'))
- labels: int32 [32768], P(('row', 'col')), may hold values from 0 to 1, as said below
- source_id: int32 [32768], P(('row', 'col')), may hold values from 0 to 32767, as said below
Outputs:
- proof: float32 [32768], P(('row', 'col'))
- mmd_value: float32 [], replicated
Inputs may be any that keep to these rules, and one draw needn't show every extreme that they name: `labels`: exactly 16384 samples carry 1. `source_id`: every sample id appears once; at a position of grid block b (positions b * 256 to (b + 1) * 256 - 1) the id's remainder modulo 256, divided by 2 and rounded down, equals b.
All inputs are finite; a program needn't handle non-finite values.
Results may differ from a plain program's by a relative error of at most 0.00007.
Values sent between devices are 32-bit elements; how exact they have to be, the bound alone decides.
A program may use at most 128 MiB of HBM per device.

v0:
```python
import jax
import jax.numpy as jnp
from jax import lax
from jax.sharding import PartitionSpec as P


def kernel_sum(query_rows, query_norm, key_rows, key_sign):
    key_norm = jnp.sum(key_rows * key_rows, axis=1)
    inner_prod = lax.dot_general(
        query_rows,
        key_rows,
        (((1,), (1,)), ((), ())),
        precision=lax.Precision.HIGHEST,
        preferred_element_type=jnp.float32,
    )
    sq_dist = query_norm[:, None] + key_norm[None, :] - 2.0 * inner_prod
    kernel = jnp.exp(sq_dist * (-1.0 / 200.0))
    return jnp.dot(
        kernel, key_sign, precision=lax.Precision.HIGHEST, preferred_element_type=jnp.float32
    )


def make_adder(query_emb, query_norm, key_piece):
    return kernel_sum(query_emb, query_norm, key_piece[0], key_piece[1])


def local(embeddings, labels, source_id):
    row_count = lax.axis_size("row")
    col_count = lax.axis_size("col")
    blocks_total = row_count * col_count
    block_rows = embeddings.shape[0]
    feature_dim = embeddings.shape[1]
    per_peer = block_rows // blocks_total
    half_count = block_rows * blocks_total // 2
    factor = 1000.0 / half_count
    set_sign = (1 - 2 * labels).astype(jnp.float32)
    picked = source_id // block_rows * per_peer + source_id % per_peer
    arrived, arrived_sign = (
        lax.all_to_all(
            embeddings.reshape(blocks_total, per_peer, feature_dim),
            ("row", "col"),
            split_axis=0,
            concat_axis=0,
            tiled=True,
        ),
        lax.all_to_all(
            set_sign.reshape(blocks_total, per_peer),
            ("row", "col"),
            split_axis=0,
            concat_axis=0,
            tiled=True,
        ),
    )
    local_emb = arrived.reshape(block_rows, feature_dim)[picked]
    local_sign = arrived_sign.reshape(block_rows)[picked]
    query_emb, query_sign = (
        lax.all_gather(local_emb, "col", axis=0, tiled=True),
        lax.all_gather(local_sign, "col", axis=0, tiled=True),
    )
    query_norm = jnp.sum(query_emb * query_emb, axis=1)
    partial_value = make_adder(
        query_emb,
        query_norm,
        (
            lax.all_gather(local_emb, "row", axis=0, tiled=True),
            lax.all_gather(local_sign, "row", axis=0, tiled=True),
        ),
    )
    scaled = partial_value * factor
    summed = lax.psum_scatter(scaled, "col", scatter_dimension=0, tiled=True)
    mmd_total = lax.psum(jnp.sum(local_sign * summed), ("row", "col"))
    mmd_value = mmd_total * (1.0 / half_count)
    return (summed, mmd_value)


def solution(mesh):
    return jax.shard_map(
        local,
        mesh=mesh,
        in_specs=(P(("row", "col"), None), P(("row", "col")), P(("row", "col"))),
        out_specs=(P(("row", "col")), P()),
        check_vma=False,
    )
```

profile of v0, /device:TPU:1, one launch (start us, length us, event | category | flops | bytes accessed | tf_op | source)
XLA Modules:
  0.0 442.0 jit_solution(15137807348988917067)
XLA Ops:
  7.2 2.5 reshape.20
  9.6 11.5 %all-to-all-start = ((f32[128,2,768]{2,1,0:T(2,128)}), f32[128,2,768]{2,1,0:T(2,128)S(1)}, u32[]{:S(2)}, u32[]{:S(2)}) async-start(f32[128,2,768]{2,1,0:T(2,128)} %reshape.20), calls=%async_computation | async-start | bytes 1572864 | tf_op jit(solution)/shard_map/all_to_all | solution.py:39
  21.1 0.0 all-gather.9.cloned.1.call-start
  21.2 0.7 compare_select_fusion
  21.9 15.2 %all-to-all-done = f32[128,2,768]{2,1,0:T(2,128)S(1)} async-done(((f32[128,2,768]{2,1,0:T(2,128)}), f32[128,2,768]{2,1,0:T(2,128)S(1)}, u32[]{:S(2)}, u32[]{:S(2)}) %all-to-all-start) | async-done | bytes 786464 | tf_op jit(solution)/shard_map/all_to_all | solution.py:39
  37.1 0.5 reshape.21
  37.7 2.0 gather_fusion
  39.6 0.0 all-gather.9.cloned.1.call-update
  39.6 0.0 all-gather.7.cloned.1.call-start
  39.7 0.7 all-gather.7.cloned.1.call-update
  40.4 0.7 subtract_convert_fusion
  41.1 0.8 all_to_all.10
  41.8 4.8 %all-to-all-start.1 = ((f32[128,1,2]{2,1,0:T(1,128)}), f32[128,1,2]{2,1,0:T(1,128)S(1)}, u32[]{:S(2)}, u32[]{:S(2)}) async-start(f32[128,1,2]{2,1,0:T(1,128)} %bitcast), calls=%async_computation.1 | async-start | bytes 131072 | tf_op jit(solution)/shard_map/all_to_all | solution.py:46
  46.7 1.2 dynamic-slice
  48.6 7.8 %all-to-all-done.1 = f32[128,1,2]{2,1,0:T(1,128)S(1)} async-done(((f32[128,1,2]{2,1,0:T(1,128)}), f32[128,1,2]{2,1,0:T(1,128)S(1)}, u32[]{:S(2)}, u32[]{:S(2)}) %all-to-all-start.1) | async-done | bytes 1056 | tf_op jit(solution)/shard_map/all_to_all | solution.py:46
  56.4 0.5 broadcast.36
  56.9 0.8 reduce.3
  57.7 0.1 reshape.22
  57.8 1.9 gather_fusion.1
  59.8 9.6 %all-gather.3 = f32[8,1,256]{2,1,0:T(1,128)S(1)} all-gather(f32[1,1,256]{2,1,0:T(1,128)S(1)} %bitcast.11), channel_id=4, replica_groups=mesh['row'=8,'col'=16] {'row'}, dimensions={0}, use_global_device_ids=true | all-gather | bytes 9216 | tf_op jit(solution)/shard_map/all_gather | solution.py:66
  69.4 8.9 %all-gather.9.cloned.1.call-done = f32[2048,768]{1,0:T(8,128)} async-done(((f32[256,768]{1,0:T(8,128)}), f32[2048,768]{1,0:T(8,128)}) %all-gather.9.cloned.1.call-update) | async-done | bytes 6291472 | tf_op jit(solution)/shard_map/all_gather | solution.py:65
  78.3 3.3 multiply_reduce_fusion.1
  81.6 88.2 %all-gather.7.cloned.1.call-done = f32[4096,768]{1,0:T(8,128)} async-done(((f32[256,768]{1,0:T(8,128)}), f32[4096,768]{1,0:T(8,128)}) %all-gather.7.cloned.1.call-update) | async-done | bytes 12582928 | tf_op jit(solution)/shard_map/all_gather | solution.py:57
  169.8 0.0 copy-start
  169.8 87.4 %fusion.13 = f32[4096,2048]{1,0:T(8,128)} fusion(f32[4096,768]{1,0:T(8,128)} %all-gather.7.cloned.1.call-done, f32[2048,768]{1,0:T(8,128)} %all-gather.9.cloned.1.call-done), kind=kOutput, calls=%fused_computation.28 | convolution fusion | flops 77309411328 | bytes 52428800 | tf_op jit(solution)/shard_map/dot_general | solution.py:9
  257.2 0.0 copy-done
  257.2 0.9 multiply_reduce_fusion
  258.1 38.8 %fusion = f32[1,4096]{1,0:T(1,128)S(1)} fusion(f32[2048,1]{0,1:T(1,128)S(1)} %bitcast.12, f32[4096,2048]{1,0:T(8,128)} %fusion.13, f32[2048]{0:T(1024)S(1)} %multiply_reduce_fusion.1, f32[4096]{0:T(1024)S(1)} %multiply_reduce_fusion), kind=kOutput, calls=%fused_computation.2 | convolution fusion | flops 134217728 | bytes 33603584 | tf_op jit(solution)/shard_map/dot_general | solution.py:18
  296.9 58.2 %all-reduce = f32[4096]{0:T(1024)S(1)} all-reduce(f32[4096]{0:T(1024)S(1)} %broadcast_multiply_fusion), channel_id=5, replica_groups=mesh['row'=8,'col'=16] {'col'}, use_global_device_ids=true, to_apply=%region_2.3.clone | all-reduce | flops 4096 | bytes 32768
  355.1 1.2 multiply_reduce_fusion.2
  356.4 77.0 %psum.7 = f32[]{:T(128)} all-reduce(f32[]{:T(128)} %get-tuple-element.2), channel_id=1, replica_groups=mesh['row'=8,'col'=16] {'row','col'}, use_global_device_ids=true, to_apply=%region_4.5 | all-reduce | flops 1 | bytes 8 | tf_op jit(solution)/shard_map/psum | solution.py:71
  (2 shorter events, 0.0 us)
Async XLA Ops:
  9.6 27.5 %all-to-all-start = ((f32[128,2,768]{2,1,0:T(2,128)}), f32[128,2,768]{2,1,0:T(2,128)S(1)}, u32[]{:S(2)}, u32[]{:S(2)}) async-start(f32[128,2,768]{2,1,0:T(2,128)} %reshape.20), calls=%async_computation | async-start | bytes 1572864 | tf_op jit(solution)/shard_map/all_to_all | solution.py:39
  21.1 57.2 %all-gather.9.cloned.1.call-start = ((), (), s32[]{:S(2)}) async-start(), calls=%async_computation.3 | async-start | bytes 7077888 | tf_op jit(solution)/shard_map/all_gather | solution.py:65
  39.6 130.2 %all-gather.7.cloned.1.call-start = ((), (), s32[]{:S(2)}) async-start(), calls=%async_computation.2 | async-start | bytes 13369344 | tf_op jit(solution)/shard_map/all_gather | solution.py:57
  41.8 14.5 %all-to-all-start.1 = ((f32[128,1,2]{2,1,0:T(1,128)}), f32[128,1,2]{2,1,0:T(1,128)S(1)}, u32[]{:S(2)}, u32[]{:S(2)}) async-start(f32[128,1,2]{2,1,0:T(1,128)} %bitcast), calls=%async_computation.1 | async-start | bytes 131072 | tf_op jit(solution)/shard_map/all_to_all | solution.py:46
  169.8 87.4 %copy-start = (f32[4096,768]{1,0:T(8,128)S(1)}, f32[4096,768]{1,0:T(8,128)}, u32[]{:S(2)}) copy-start(f32[4096,768]{1,0:T(8,128)} %all-gather.7.cloned.1.call-done) | copy-start | bytes 37748740
Sparse Core Ops, SparseCore 0:
  39.8 38.5 all-gather.8
  80.5 89.2 all-gather.6
where the time goes:
time: 442 us
  blocking collectives  145 us (33%)
  matrix products  126 us (29%)
  waiting for transfers between devices  121 us (27%)
  between operations  16.5 us (4%)
  starting transfers between devices  16.4 us (4%)
  local copies, waits for them, and re-layouts  9.57 us (2%)
  other arithmetic  7.59 us (2%)
    all_gather x1, waiting for transfers between devices, local(): lax.all_gather(local_emb, 'col', axis=0, tiled=True)  88.2 us
    dot_general x1, matrix products, kernel_sum(): lax.dot_general(query_rows, key_rows, (((1,), (1,)), ((), ())), precision...  87.4 us
    psum x1, blocking collectives, local(): mmd_total = lax.psum(jnp.sum(local_sign * summed), ('row', 'col'))  77 us
    unnamed x1, blocking collectives  58.2 us
    dot_general x1, matrix products, kernel_sum(): jnp.dot(kernel, key_sign, precision=lax.Precision.HIGHEST, preferred_elem...  38.8 us
    all_to_all x1, waiting for transfers between devices, local(): lax.all_to_all(embeddings.reshape(blocks_total, per_peer, feature_dim), (...  15.2 us
    all_to_all x1, starting transfers between devices, local(): lax.all_to_all(embeddings.reshape(blocks_total, per_peer, feature_dim), (...  11.5 us
    all_gather x1, blocking collectives, local(): lax.all_gather(local_sign, 'row', axis=0, tiled=True)  9.64 us
  transfers between devices with their start and end apart: 4, of which 4 were waited for; matrix products, arithmetic and copies ran while one was open for 2% of the time, Pallas kernels for 0%

commit v1 on v0

v1 whole, which is shorter than its diff:
```python
import functools
import math

import jax
import jax.numpy as jnp
from jax import lax
from jax.experimental import pallas as pl
from jax.experimental.pallas import tpu as pltpu
from jax.sharding import PartitionSpec as P

MESH = pl.DeviceIdType.MESH
D = 768
ROWS = 256
AUX = 8
CHUNKS = 4
CORES = 2
ROWS_MESH = 8
COLS_MESH = 16
HALF_COUNT = 16384
SCALE = math.sqrt(2.0 * math.log2(math.e) / 200.0)

DIRS = [(1, 0, 0), (3, 0, 0), (0, 1, 0), (0, 3, 0), (0, 0, 1), (0, 0, 3)]
EDGES = [
    ((0, 0, 0), (3, 0, 0)), ((0, 0, 0), (1, 0, 0)), ((0, 0, 0), (0, 1, 0)),
    ((0, 0, 0), (0, 0, 1)), ((1, 0, 0), (2, 0, 0)), ((0, 1, 0), (0, 1, 3)),
    ((0, 0, 1), (0, 0, 2)), ((3, 0, 0), (3, 3, 0)), ((2, 0, 0), (2, 3, 0)),
    ((0, 1, 3), (0, 2, 3)), ((0, 2, 3), (0, 2, 2)),
]
ORDER = [
    (0, 0, 0), (3, 0, 0), (1, 0, 0), (0, 1, 0), (0, 0, 1), (0, 1, 3), (3, 3, 0),
    (0, 0, 2), (2, 0, 0), (0, 2, 3), (2, 3, 0), (0, 2, 2),
]
COUNT = len(ORDER)
SLOTS = CORES * COUNT
INDEX = {e: i for i, e in enumerate(ORDER)}
STEP = ROWS // CHUNKS


def minus(a, b):
    return tuple((u - v) % 4 for u, v in zip(a, b))


def pair_table():
    seen, table = set(), []
    for j in range(COUNT):
        full, half = [], []
        for i in range(j):
            diff = minus(ORDER[j], ORDER[i])
            kind = min(diff, minus((0, 0, 0), diff))
            if kind in seen:
                continue
            seen.add(kind)
            if all(v % 2 == 0 for v in kind):
                half.append((i, [t for t in range(3) if diff[t] == 2][0]))
            else:
                full.append(i)
        table.append((full, half))
    return table


CHILDREN = {i: [INDEX[w] for u, w in EDGES if INDEX[u] == i] for i in range(COUNT)}
PARENT = {INDEX[w]: INDEX[u] for u, w in EDGES}
PAIRS = pair_table()


def span(chunk):
    start = chunk * STEP
    return pl.ds(start, STEP + (AUX if chunk == CHUNKS - 1 else 0))


def product(a, b):
    dims = (((1,), (1,)), ((), ()))

    def dot(u, v):
        return lax.dot_general(u, v, dims, preferred_element_type=jnp.float32)

    return dot(a[:, :D], b[:, :D]) + dot(a[:, :D], b[:, D:]) + dot(a[:, D:], b[:, :D])


def kernel(
    emb, lab, src, out, mmd,
    raw, split, cols, row_acc, col_acc, part, part_in, every,
    load_sem, tree_send, tree_recv, sib_send, sib_recv, part_send, part_recv,
    col_send, col_recv, row_send, row_recv,
):
    row, col = lax.axis_index("row"), lax.axis_index("col")
    place = (col // 4, col % 4, row // 2)
    core = row % 2
    me = row * COLS_MESH + col

    def device(offset, flip=False):
        x, y, z = ((p + o) % 4 for p, o in zip(place, offset))
        c = (1 - core) if flip else core
        return (z * 2 + c, x * 4 + y)

    load = pltpu.make_async_copy(emb, raw.at[0, pl.ds(0, ROWS)], load_sem)
    load.start()
    barrier = pltpu.get_barrier_semaphore()
    for offset in DIRS:
        pl.semaphore_signal(barrier, inc=1, device_id=device(offset), device_id_type=MESH)
    pl.semaphore_signal(barrier, inc=1, device_id=device((0, 0, 0), True), device_id_type=MESH)

    load.wait()
    y = raw[0, pl.ds(0, ROWS)] * SCALE
    minus_half = -0.5 * jnp.sum(y * y, axis=1, keepdims=True)
    norm_row = jnp.transpose(jnp.broadcast_to(minus_half, (ROWS, 128)))[0:1]
    sign_row = (1 - 2 * lab[...]).astype(jnp.float32)
    aux = jnp.concatenate([norm_row, sign_row, jnp.zeros((AUX - 2, ROWS), jnp.float32)], axis=0)
    raw[0, pl.ds(ROWS, AUX)] = jnp.concatenate([aux, jnp.zeros((AUX, D - ROWS), jnp.float32)], axis=1)
    pl.semaphore_wait(barrier, 7)

    sent = []

    def relay(i, chunk):
        for w in CHILDREN[i]:
            back = minus(ORDER[i], ORDER[w])
            copy = pltpu.make_async_remote_copy(
                src_ref=raw.at[2 * i, span(chunk)],
                dst_ref=raw.at[2 * w, span(chunk)],
                send_sem=tree_send.at[w, chunk],
                recv_sem=tree_recv.at[w, chunk],
                device_id=device(back),
                device_id_type=MESH,
            )
            copy.start()
            sent.append(copy)

    def arrive(i, chunk):
        pltpu.make_async_remote_copy(
            src_ref=raw.at[2 * i, span(chunk)],
            dst_ref=raw.at[2 * i, span(chunk)],
            send_sem=tree_send.at[i, chunk],
            recv_sem=tree_recv.at[i, chunk],
            device_id=device(minus(ORDER[i], ORDER[PARENT[i]])),
            device_id_type=MESH,
        ).wait_recv()

    sibling = []

    def share(i):
        copy = pltpu.make_async_remote_copy(
            src_ref=raw.at[2 * i],
            dst_ref=raw.at[2 * i + 1],
            send_sem=sib_send.at[i],
            recv_sem=sib_recv.at[i],
            device_id=device((0, 0, 0), True),
            device_id_type=MESH,
        )
        copy.start()
        sent.append(copy)
        sibling.append(copy)

    def prepare(slot):
        @pl.loop(0, ROWS // 64)
        def _(t):
            rows = pl.ds(pl.multiple_of(t * 64, 64), 64)
            y = raw[slot, rows] * SCALE
            high = y.astype(jnp.bfloat16)
            split[slot, rows, :D] = high
            split[slot, rows, D:] = (y - high.astype(jnp.float32)).astype(jnp.bfloat16)
        if slot % 2 == 0:
            aux = raw[slot, pl.ds(ROWS, AUX), :ROWS]
            cols[slot // 2] = jnp.transpose(jnp.concatenate([aux] * (128 // AUX), axis=0))

    def work(i, slots, both):
        a = split[2 * i]
        norm_i, sign_i = cols[i, :, 0:1], cols[i, :, 1:2]
        for slot in slots:
            g = product(a, split[slot])
            aux = raw[slot, pl.ds(ROWS, AUX), :ROWS]
            e = jnp.exp2(g + norm_i + aux[0:1])
            q = e * aux[1:2]
            row_acc[i] += q[:, :128] + q[:, 128:]
            if both:
                col_acc[slot] += jnp.sum((e * sign_i).reshape(ROWS // 8, 8, ROWS), axis=0)

    for chunk in range(CHUNKS):
        relay(0, chunk)
    share(0)
    row_acc[...] = jnp.zeros_like(row_acc)
    col_acc[...] = jnp.zeros_like(col_acc)
    prepare(0)
    work(0, [0], False)
    sibling[0].wait_recv()
    prepare(1)
    work(0, [1], False)

    def take(i):
        for slot in (2 * i, 2 * i + 1):
            if slot % 2:
                sib_wait(i)
            prepare(slot)

    def sib_wait(i):
        pltpu.make_async_remote_copy(
            src_ref=raw.at[2 * i],
            dst_ref=raw.at[2 * i + 1],
            send_sem=sib_send.at[i],
            recv_sem=sib_recv.at[i],
            device_id=device((0, 0, 0), True),
            device_id_type=MESH,
        ).wait_recv()

    def pairs(i):
        full, half = PAIRS[i]
        if full:
            digits = sum(f << (4 * t) for t, f in enumerate(full))

            @pl.loop(0, len(full))
            def _(t):
                b = lax.shift_right_logical(jnp.int32(digits), jnp.int32(4 * t)) & 15
                work(i, [2 * b, 2 * b + 1], True)
        for b, axis in half:
            work(i, [2 * b + place[axis] // 2], True)

    def arrivals(level, chunk):
        for i in level:
            arrive(i, chunk)
            relay(i, chunk)

    levels = [[1, 2, 3, 4], [5, 6, 7, 8], [9, 10], [11]]
    for chunk in range(CHUNKS):
        arrivals(levels[0], chunk)
        if chunk >= 1:
            arrivals([5, 6], chunk - 1)
        if chunk >= 2:
            arrivals([9], chunk - 2)
    for i in levels[0]:
        share(i)
    for i in (1, 2):
        take(i)
        pairs(i)
    arrivals([5, 6], CHUNKS - 1)
    share(5)
    share(6)
    arrivals([8], 0)
    for i in (3, 4):
        take(i)
        pairs(i)
    arrivals([8], 1)
    arrivals([9], CHUNKS - 2)
    arrivals([9], CHUNKS - 1)
    for i in (5, 6):
        take(i)
        pairs(i)
    arrivals([8], 2)
    arrivals([8], 3)
    for i in (7, 9, 10, 11):
        if i in (9,):
            share(9)
            share(8)
            continue
        for chunk in range(CHUNKS):
            arrive(i, chunk)
        share(i)
    for i in (7, 8, 9, 10, 11):
        take(i)
        pairs(i)

    home = []
    for slot in range(SLOTS):
        i = slot // 2
        total = jnp.sum(col_acc[slot], axis=0, keepdims=True)
        if slot % 2 == 0:
            total = total + jnp.sum(jnp.transpose(row_acc[i]), axis=0, keepdims=True)
        part[slot] = total
        if slot:
            copy = pltpu.make_async_remote_copy(
                src_ref=part.at[slot],
                dst_ref=part_in.at[slot],
                send_sem=part_send.at[slot],
                recv_sem=part_recv.at[slot],
                device_id=device(ORDER[i], slot % 2 == 1),
                device_id_type=MESH,
            )
            copy.start()
            home.append(copy)
    proof = part[0]
    for t, copy in enumerate(home):
        copy.wait_recv()
        proof = proof + part_in[t + 1]
    proof = proof * (1000.0 / HALF_COUNT)
    here = jnp.sum(proof * sign_row, axis=1, keepdims=True)
    every[pl.ds(me, 1), :] = jnp.concatenate([proof, jnp.broadcast_to(here, (1, 128))], axis=1)

    copies = []
    for k in range(1, COLS_MESH):
        copy = pltpu.make_async_remote_copy(
            src_ref=every.at[pl.ds(me, 1)],
            dst_ref=every.at[pl.ds(me, 1)],
            send_sem=col_send.at[k],
            recv_sem=col_recv.at[k],
            device_id=(row, (col + k) % COLS_MESH),
            device_id_type=MESH,
        )
        copy.start()
        copies.append(copy)
    for k in range(1, COLS_MESH):
        other = row * COLS_MESH + (col + COLS_MESH - k) % COLS_MESH
        pltpu.make_async_remote_copy(
            src_ref=every.at[pl.ds(other, 1)],
            dst_ref=every.at[pl.ds(other, 1)],
            send_sem=col_send.at[k],
            recv_sem=col_recv.at[k],
            device_id=(row, (col + k) % COLS_MESH),
            device_id_type=MESH,
        ).wait_recv()
    for k in range(1, ROWS_MESH):
        block = pl.ds(pl.multiple_of(row * COLS_MESH, COLS_MESH), COLS_MESH)
        copy = pltpu.make_async_remote_copy(
            src_ref=every.at[block],
            dst_ref=every.at[block],
            send_sem=row_send.at[k],
            recv_sem=row_recv.at[k],
            device_id=((row + k) % ROWS_MESH, col),
            device_id_type=MESH,
        )
        copy.start()
        copies.append(copy)
    for k in range(1, ROWS_MESH):
        other = (row + ROWS_MESH - k) % ROWS_MESH
        block = pl.ds(pl.multiple_of(other * COLS_MESH, COLS_MESH), COLS_MESH)
        pltpu.make_async_remote_copy(
            src_ref=every.at[block],
            dst_ref=every.at[block],
            send_sem=row_send.at[k],
            recv_sem=row_recv.at[k],
            device_id=((row + k) % ROWS_MESH, col),
            device_id_type=MESH,
        ).wait_recv()

    proofs = every[:, :ROWS]
    lane = lax.broadcasted_iota(jnp.int32, proofs.shape, 1)
    first = jnp.sum(jnp.where(lane == 2 * me, proofs, 0.0), axis=1, keepdims=True)
    second = jnp.sum(jnp.where(lane == 2 * me + 1, proofs, 0.0), axis=1, keepdims=True)
    ids = src[...]
    owner = lax.broadcasted_iota(jnp.int32, proofs.shape, 0)
    value = jnp.where((ids & 1) == 0, first, second)
    out[...] = jnp.sum(jnp.where(owner == ids // ROWS, value, 0.0), axis=0, keepdims=True)
    total = jnp.sum(every[:, pl.ds(ROWS, 128)], axis=0, keepdims=True)
    mmd[...] = total * (1.0 / HALF_COUNT)
    for copy in sent + home + copies:
        copy.wait_send()


def local(embeddings, labels, source_id):
    vmem = pl.BlockSpec(memory_space=pltpu.VMEM)
    dma = pltpu.SemaphoreType.DMA
    f32 = jnp.float32
    proof, mmd = pl.pallas_call(
        kernel,
        out_shape=[
            jax.ShapeDtypeStruct((1, ROWS), f32),
            jax.ShapeDtypeStruct((1, 128), f32),
        ],
        in_specs=[pl.BlockSpec(memory_space=pl.ANY), vmem, vmem],
        out_specs=[vmem, vmem],
        scratch_shapes=[
            pltpu.VMEM((SLOTS, ROWS + AUX, D), f32),
            pltpu.VMEM((SLOTS, ROWS, 2 * D), jnp.bfloat16),
            pltpu.VMEM((COUNT, ROWS, 128), f32),
            pltpu.VMEM((COUNT, ROWS, 128), f32),
            pltpu.VMEM((SLOTS, 8, ROWS), f32),
            pltpu.VMEM((SLOTS, 1, ROWS), f32),
            pltpu.VMEM((SLOTS, 1, ROWS), f32),
            pltpu.VMEM((ROWS_MESH * COLS_MESH, ROWS + 128), f32),
            dma,
            dma((COUNT, CHUNKS)),
            dma((COUNT, CHUNKS)),
            dma((COUNT,)),
            dma((COUNT,)),
            dma((SLOTS,)),
            dma((SLOTS,)),
            dma((COLS_MESH,)),
            dma((COLS_MESH,)),
            dma((ROWS_MESH,)),
            dma((ROWS_MESH,)),
        ],
        compiler_params=pltpu.CompilerParams(
            collective_id=0, has_side_effects=True, vmem_limit_bytes=56 * 2**20
        ),
    )(embeddings, labels.reshape(1, ROWS), source_id.reshape(1, ROWS))
    return proof.reshape(ROWS), mmd[0, 0]


def solution(mesh):
    return jax.shard_map(
        local,
        mesh=mesh,
        in_specs=(P(("row", "col"), None), P(("row", "col")), P(("row", "col"))),
        out_specs=(P(("row", "col")), P()),
        check_vma=False,
    )
```

time: 442 us -> 104 us (0.24)
  blocking collectives: 145 us -> 0 us
  matrix products: 126 us -> 0 us
  waiting for transfers between devices: 121 us -> 0 us
  Pallas kernels: 0 us -> 100 us
  starting transfers between devices: 16.4 us -> 0 us
  between operations: 16.5 us -> 1.81 us
  local copies, waits for them, and re-layouts: 9.57 us -> 1.29 us
  other arithmetic: 7.59 us -> 0 us
    dot_general x2 -> x0, matrix products: 126 us -> none  [the longest x1 87.4 us: kernel_sum(): lax.dot_general(query_rows, key_rows, (((1,), (1,)), ((), ())), precision...]
    pallas_call x0 -> x1, Pallas kernels: none -> 100 us  [local(): pl.pallas_call(kernel, out_shape=[jax.ShapeDtypeStruct((1, ROWS), f32), j...]
    all_gather x2 -> x0, waiting for transfers between devices: 97.1 us -> none  [the longest x1 88.2 us: local(): lax.all_gather(local_emb, 'col', axis=0, tiled=True)]
    psum x1 -> x0, blocking collectives: 77 us -> none  [local(): mmd_total = lax.psum(jnp.sum(local_sign * summed), ('row', 'col'))]
    unnamed x1 -> x0, blocking collectives: 58.2 us -> none
    all_to_all x2 -> x0, waiting for transfers between devices: 23 us -> none  [the longest x1 15.2 us: local(): lax.all_to_all(embeddings.reshape(blocks_total, per_peer, feature_dim), (...]
    all_to_all x2 -> x0, starting transfers between devices: 16.3 us -> none  [the longest x1 11.5 us: local(): lax.all_to_all(embeddings.reshape(blocks_total, per_peer, feature_dim), (...]
    all_gather x1 -> x0, blocking collectives: 9.64 us -> none  [local(): lax.all_gather(local_sign, 'row', axis=0, tiled=True)]
  transfers between devices with their start and end apart: 4 -> 0, of which waited for: 4 -> 0; matrix products, arithmetic and copies ran while one was open for 2% -> 0% of each run, Pallas kernels for 0% -> 0%
where the time goes in v1:
time: 104 us
  Pallas kernels  100 us (96%)
  between operations  1.81 us (2%)
  local copies, waits for them, and re-layouts  1.29 us (1%)
    pallas_call x1, Pallas kernels, local(): pl.pallas_call(kernel, out_shape=[jax.ShapeDtypeStruct((1, ROWS), f32), j...  100 us

profile of v1, /device:TPU:1, one launch (start us, length us, event | category | flops | bytes accessed | tf_op | source)
XLA Modules:
  0.0 103.5 jit_solution(8414340931301711021)
XLA Ops:
  0.6 100.4 %shard_map.50 = (f32[1,256]{1,0:T(1,128)}, f32[1,128]{1,0:T(1,128)}) custom-call(f32[256,768]{1,0:T(8,128)} %emb.1, s32[1,256]{1,0:T(1,128)} %bitcast.5, s32[1,256]{1,0:T(1,128)} %bitcast.6), custom_call_target="tpu_custom_call" | custom-call | tf_op jit(solution)/shard_map/pallas_call | solution.py:350
  101.0 0.0 copy-start
  101.1 0.7 copy-done
  101.7 0.0 copy-start.1
  101.7 0.6 copy.7
  102.3 0.1 copy-done.1
Async XLA Ops:
  101.0 0.7 copy-start
  101.7 0.6 copy-start.1

commit v2 on v0

v2 whole, which is shorter than its diff:
```python
import math

import jax
import jax.numpy as jnp
from jax import lax
from jax.experimental import pallas as pl
from jax.experimental.pallas import tpu as pltpu
from jax.sharding import PartitionSpec as P

MESH = pl.DeviceIdType.MESH
D = 768
ROWS = 256
AUX = 8
CORES = 2
ROWS_MESH = 8
COLS_MESH = 16
HALF_COUNT = 16384
SCALE = math.sqrt(2.0 * math.log2(math.e) / 200.0)

CHUNKS = 4
ORDER = [(0, 0, 0), (0, 0, 1), (0, 0, 3), (0, 3, 0), (3, 0, 0), (0, 1, 3), (1, 3, 0), (0, 0, 2), (0, 1, 2), (1, 2, 0), (2, 0, 0), (2, 2, 0)]
EDGES = [((0, 0, 0), (3, 0, 0)), ((0, 0, 0), (0, 0, 3)), ((0, 0, 0), (0, 3, 0)), ((0, 0, 0), (0, 0, 1)), ((0, 0, 3), (0, 1, 3)), ((0, 3, 0), (1, 3, 0)), ((3, 0, 0), (2, 0, 0)), ((0, 0, 1), (0, 0, 2)), ((0, 1, 3), (0, 1, 2)), ((1, 3, 0), (1, 2, 0)), ((1, 2, 0), (2, 2, 0))]
PLAN = [
    ('fwd', 1, 0),
    ('fwd', 2, 0),
    ('fwd', 3, 0),
    ('fwd', 4, 0),
    ('fwd', 1, 1),
    ('fwd', 2, 1),
    ('fwd', 3, 1),
    ('fwd', 4, 1),
    ('fwd', 5, 0),
    ('fwd', 6, 0),
    ('fwd', 1, 2),
    ('fwd', 2, 2),
    ('fwd', 3, 2),
    ('fwd', 4, 2),
    ('fwd', 5, 1),
    ('fwd', 6, 1),
    ('fwd', 1, 3),
    ('share', 1),
    ('fwd', 2, 3),
    ('share', 2),
    ('fwd', 3, 3),
    ('share', 3),
    ('fwd', 4, 3),
    ('share', 4),
    ('fwd', 5, 2),
    ('fwd', 6, 2),
    ('take', 1),
    ('full', 1, (0,)),
    ('take', 2),
    ('half', 2, (1,)),
    ('fwd', 9, 0),
    ('take', 3),
    ('full', 3, (0, 1)),
    ('fwd', 5, 3),
    ('share', 5),
    ('fwd', 6, 3),
    ('share', 6),
    ('full', 3, (2,)),
    ('take', 4),
    ('full', 4, (0, 1)),
    ('fwd', 9, 1),
    ('full', 4, (2, 3)),
    ('take', 5),
    ('full', 5, (1, 3)),
    ('fwd', 9, 2),
    ('full', 5, (4,)),
    ('take', 6),
    ('full', 6, (1, 2, 4, 5)),
    ('share', 7),
    ('share', 8),
    ('fwd', 9, 3),
    ('share', 9),
    ('share', 10),
    ('take', 7),
    ('full', 7, (4, 6)),
    ('take', 8),
    ('full', 8, (4, 6)),
    ('half', 8, (3,)),
    ('take', 9),
    ('full', 9, (0, 1)),
    ('share', 11),
    ('full', 9, (5,)),
    ('half', 9, (4,)),
    ('take', 10),
    ('full', 10, (1, 5, 6, 8)),
    ('half', 10, (0, 7)),
    ('take', 11),
    ('full', 11, (1, 5)),
    ('half', 11, (7, 10)),
]

DIRS = [(1, 0, 0), (3, 0, 0), (0, 1, 0), (0, 3, 0), (0, 0, 1), (0, 0, 3)]
COUNT = len(ORDER)
SLOTS = CORES * COUNT
INDEX = {e: i for i, e in enumerate(ORDER)}
STEP = ROWS // CHUNKS
CHILDREN = {i: [INDEX[w] for u, w in EDGES if INDEX[u] == i] for i in range(COUNT)}
PARENT = {INDEX[w]: INDEX[u] for u, w in EDGES}
FIRST_SEM = {}
SEMS = 0
for _i in range(1, COUNT):
    FIRST_SEM[_i] = SEMS
    SEMS += CHUNKS if CHILDREN[_i] else 1


def minus(a, b):
    return tuple((u - v) % 4 for u, v in zip(a, b))


def span(chunk):
    start = chunk * STEP
    return pl.ds(start, STEP + (AUX if chunk == CHUNKS - 1 else 0))


def product(a, b):
    dims = (((1,), (1,)), ((), ()))

    def dot(u, v):
        return lax.dot_general(u, v, dims, preferred_element_type=jnp.float32)

    return dot(a[:, :D], b[:, :D]) + dot(a[:, :D], b[:, D:]) + dot(a[:, D:], b[:, :D])


def kernel(
    emb, lab, src, out,
    raw, split, cols, row_acc, col_acc, part, part_in, stage, final,
    load_sem, tree_send, tree_recv, sib_send, sib_recv, part_send, part_recv,
    row_send, row_recv, col_send, col_recv,
):
    row, col = lax.axis_index("row"), lax.axis_index("col")
    place = (col // 4, col % 4, row // 2)
    core = row % 2
    me = row * COLS_MESH + col

    def device(offset, flip=False):
        x, y, z = ((p + o) % 4 if o else p for p, o in zip(place, offset))
        c = (1 - core) if flip else core
        return (z * 2 + c, x * 4 + y)

    other_core = device((0, 0, 0), True)

    def remote(source, target, send, recv, to):
        return pltpu.make_async_remote_copy(
            src_ref=source, dst_ref=target, send_sem=send, recv_sem=recv,
            device_id=to, device_id_type=MESH,
        )

    load = pltpu.make_async_copy(emb, raw.at[0, pl.ds(0, ROWS)], load_sem)
    load.start()
    barrier = pltpu.get_barrier_semaphore()
    for offset in DIRS:
        pl.semaphore_signal(barrier, inc=1, device_id=device(offset), device_id_type=MESH)
    pl.semaphore_signal(barrier, inc=1, device_id=other_core, device_id_type=MESH)

    load.wait()
    y = raw[0, pl.ds(0, ROWS)] * SCALE
    minus_half = -0.5 * jnp.sum(y * y, axis=1, keepdims=True)
    norm_row = jnp.transpose(jnp.broadcast_to(minus_half, (ROWS, 128)))[0:1]
    sign_row = (1 - 2 * lab[...]).astype(jnp.float32)
    aux = jnp.concatenate([norm_row, sign_row, jnp.zeros((AUX - 2, ROWS), jnp.float32)], axis=0)
    raw[0, pl.ds(ROWS, AUX)] = jnp.concatenate([aux, jnp.zeros((AUX, D - ROWS), jnp.float32)], axis=1)
    pl.semaphore_wait(barrier, 7)

    def relay(i, chunk):
        for w in CHILDREN[i]:
            sem = FIRST_SEM[w] + (chunk if CHILDREN[w] else 0)
            remote(
                raw.at[2 * i, span(chunk)], raw.at[2 * w, span(chunk)],
                tree_send, tree_recv.at[sem], device(minus(ORDER[i], ORDER[w])),
            ).start()

    def arrive(i, chunk):
        sem = FIRST_SEM[i] + (chunk if CHILDREN[i] else 0)
        rows = raw.at[2 * i, span(chunk)] if CHILDREN[i] else raw.at[2 * i]
        remote(rows, rows, tree_send, tree_recv.at[sem], other_core).wait_recv()

    def sibling(i):
        return remote(raw.at[2 * i], raw.at[2 * i + 1], sib_send, sib_recv.at[i], other_core)

    def prepare(slot):
        @pl.loop(0, ROWS // 64)
        def _(t):
            rows = pl.ds(pl.multiple_of(t * 64, 64), 64)
            y = raw[slot, rows] * SCALE
            high = y.astype(jnp.bfloat16)
            split[slot, rows, :D] = high
            split[slot, rows, D:] = (y - high.astype(jnp.float32)).astype(jnp.bfloat16)
        if slot % 2 == 0:
            aux = raw[slot, pl.ds(ROWS, AUX), :ROWS]
            cols[slot // 2] = jnp.transpose(jnp.concatenate([aux] * (128 // AUX), axis=0))

    def work(i, slots, both=True):
        a = split[2 * i]
        norm_i, sign_i = cols[i, :, 0:1], cols[i, :, 1:2]
        for slot in slots:
            g = product(a, split[slot])
            aux = raw[slot, pl.ds(ROWS, AUX), :ROWS]
            e = jnp.exp2(g + norm_i + aux[0:1])
            q = e * aux[1:2]
            row_acc[i] += q[:, :128] + q[:, 128:]
            if both:
                col_acc[slot] += jnp.sum((e * sign_i).reshape(ROWS // 8, 8, ROWS), axis=0)

    def full(i, partners):
        pairs = len(partners) // 2
        if pairs > 1:
            digits = sum(f << (4 * t) for t, f in enumerate(partners[:2 * pairs]))

            @pl.loop(0, pairs)
            def _(t):
                both = lax.shift_right_logical(jnp.int32(digits), jnp.int32(8 * t))
                b, c = both & 15, lax.shift_right_logical(both, jnp.int32(4)) & 15
                work(i, [2 * b, 2 * b + 1, 2 * c, 2 * c + 1])
        elif pairs:
            b, c = partners[:2]
            work(i, [2 * b, 2 * b + 1, 2 * c, 2 * c + 1])
        if len(partners) % 2:
            b = partners[-1]
            work(i, [2 * b, 2 * b + 1])

    def half(i, partners):
        slots = []
        for b in partners:
            diff = minus(ORDER[i], ORDER[b])
            axis = [t for t in range(3) if diff[t] == 2][0]
            slots.append(2 * b + place[axis] // 2)
        work(i, slots)

    for chunk in range(CHUNKS):
        relay(0, chunk)
    sibling(0).start()
    row_acc[...] = jnp.zeros_like(row_acc)
    col_acc[...] = jnp.zeros_like(col_acc)
    prepare(0)
    sibling(0).wait_recv()
    prepare(1)
    work(0, [0, 1], False)

    for op, i, *rest in PLAN:
        if op == "fwd":
            arrive(i, rest[0])
            relay(i, rest[0])
        elif op == "share":
            if not CHILDREN[i]:
                arrive(i, 0)
            sibling(i).start()
        elif op == "take":
            prepare(2 * i)
            sibling(i).wait_recv()
            prepare(2 * i + 1)
        elif op == "full":
            full(i, rest[0])
        else:
            half(i, rest[0])

    for slot in range(SLOTS):
        i = slot // 2
        total = jnp.sum(col_acc[slot], axis=0, keepdims=True)
        if slot % 2 == 0:
            total = total + jnp.sum(jnp.transpose(row_acc[i]), axis=0, keepdims=True)
        part[slot] = total
        if slot:
            remote(
                part.at[slot], part_in.at[slot], part_send, part_recv,
                device(ORDER[i], slot % 2 == 1),
            ).start()
    rest = pl.ds(1, SLOTS - 1)
    arrived = remote(part.at[rest], part_in.at[rest], part_send, part_recv, other_core)
    arrived.wait_recv()
    proof = part[0]
    for slot in range(1, SLOTS):
        proof = proof + part_in[slot]
    proof = proof * (1000.0 / HALF_COUNT)
    here = jnp.sum(proof * sign_row, axis=1, keepdims=True)
    stage[pl.ds(row, 1), :] = jnp.concatenate([proof, jnp.broadcast_to(here, (1, 128))], axis=1)

    for k in range(1, ROWS_MESH):
        mine = stage.at[pl.ds(row, 1)]
        remote(mine, mine, row_send, row_recv, ((row + k) % ROWS_MESH, col)).start()
    seven = remote(
        raw.at[0, pl.ds(0, ROWS_MESH - 1), pl.ds(0, ROWS + 128)],
        raw.at[0, pl.ds(0, ROWS_MESH - 1), pl.ds(0, ROWS + 128)],
        row_send, row_recv, other_core,
    )
    seven.wait_recv()
    window = jnp.where(row < ROWS_MESH // 2, stage[:, :128], stage[:, 128:256])
    column_total = jnp.sum(stage[:, 256:], axis=0, keepdims=True)
    lane = lax.broadcasted_iota(jnp.int32, (8, 128), 1)
    base = (row % 4) * 32
    window = jnp.where((lane >= base) & (lane < base + 32), window, column_total)
    block = final.at[pl.ds(pl.multiple_of(col * 8, 8), 8)]
    final[pl.ds(pl.multiple_of(col * 8, 8), 8), :] = window
    for k in range(1, COLS_MESH):
        remote(block, block, col_send, col_recv, (row, (col + k) % COLS_MESH)).start()
    fifteen = remote(
        raw.at[0, pl.ds(0, 120), pl.ds(0, 128)], raw.at[0, pl.ds(0, 120), pl.ds(0, 128)],
        col_send, col_recv, other_core,
    )
    fifteen.wait_recv()

    values = final[...]
    lane = lax.broadcasted_iota(jnp.int32, values.shape, 1)
    first = jnp.sum(jnp.where(lane == base + 2 * col, values, 0.0), axis=1, keepdims=True)
    second = jnp.sum(jnp.where(lane == base + 2 * col + 1, values, 0.0), axis=1, keepdims=True)
    ids = src[...]
    held = lax.broadcasted_iota(jnp.int32, (128, ROWS), 0)
    owner = (held % 8) * COLS_MESH + held // 8
    value = jnp.where((ids & 1) == 0, first, second)
    proofs = jnp.sum(jnp.where(owner == ids // ROWS, value, 0.0), axis=0, keepdims=True)
    unused = (base + 32) % 128
    sums = jnp.sum(jnp.where((lane == unused) & (held[:, :128] % 8 == 0), values, 0.0), axis=0, keepdims=True)
    total = jnp.sum(sums, axis=1, keepdims=True) * (1.0 / HALF_COUNT)
    out[...] = jnp.concatenate([proofs, jnp.broadcast_to(total, (1, 128))], axis=1)

    tree = raw.at[pl.ds(0, COUNT - 1)]
    remote(tree, tree, tree_send, load_sem, other_core).wait_send()
    shared = raw.at[pl.ds(0, COUNT)]
    remote(shared, shared, sib_send, load_sem, other_core).wait_send()
    arrived.wait_send()
    seven.wait_send()
    fifteen.wait_send()


def local(embeddings, labels, source_id):
    vmem = pl.BlockSpec(memory_space=pltpu.VMEM)
    dma = pltpu.SemaphoreType.DMA
    f32 = jnp.float32
    result = pl.pallas_call(
        kernel,
        out_shape=jax.ShapeDtypeStruct((1, ROWS + 128), f32),
        in_specs=[pl.BlockSpec(memory_space=pl.ANY), vmem, vmem],
        out_specs=vmem,
        scratch_shapes=[
            pltpu.VMEM((SLOTS, ROWS + AUX, D), f32),
            pltpu.VMEM((SLOTS, ROWS, 2 * D), jnp.bfloat16),
            pltpu.VMEM((COUNT, ROWS, 128), f32),
            pltpu.VMEM((COUNT, ROWS, 128), f32),
            pltpu.VMEM((SLOTS, 8, ROWS), f32),
            pltpu.VMEM((SLOTS, 1, ROWS), f32),
            pltpu.VMEM((SLOTS, 1, ROWS), f32),
            pltpu.VMEM((ROWS_MESH, ROWS + 128), f32),
            pltpu.VMEM((ROWS_MESH * COLS_MESH, 128), f32),
            dma, dma, dma((SEMS,)), dma, dma((COUNT,)), dma, dma, dma, dma, dma, dma,
        ],
        compiler_params=pltpu.CompilerParams(
            collective_id=0, has_side_effects=True, vmem_limit_bytes=56 * 2**20
        ),
    )(embeddings, labels.reshape(1, ROWS), source_id.reshape(1, ROWS))
    return result[0, :ROWS], result[0, ROWS]


def solution(mesh):
    return jax.shard_map(
        local,
        mesh=mesh,
        in_specs=(P(("row", "col"), None), P(("row", "col")), P(("row", "col"))),
        out_specs=(P(("row", "col")), P()),
        check_vma=False,
    )
```

time: 442 us -> 78.6 us (0.18)
  blocking collectives: 145 us -> 0 us
  matrix products: 126 us -> 0 us
  waiting for transfers between devices: 121 us -> 0 us
  Pallas kernels: 0 us -> 75.9 us
  starting transfers between devices: 16.4 us -> 0 us
  between operations: 16.5 us -> 0.65 us
  local copies, waits for them, and re-layouts: 9.57 us -> 1.81 us
  other arithmetic: 7.59 us -> 0 us
    dot_general x2 -> x0, matrix products: 126 us -> none  [the longest x1 87.4 us: kernel_sum(): lax.dot_general(query_rows, key_rows, (((1,), (1,)), ((), ())), precision...]
    all_gather x2 -> x0, waiting for transfers between devices: 97.1 us -> none  [the longest x1 88.2 us: local(): lax.all_gather(local_emb, 'col', axis=0, tiled=True)]
    psum x1 -> x0, blocking collectives: 77 us -> none  [local(): mmd_total = lax.psum(jnp.sum(local_sign * summed), ('row', 'col'))]
    pallas_call x0 -> x1, Pallas kernels: none -> 75.9 us  [local(): pl.pallas_call(kernel, out_shape=jax.ShapeDtypeStruct((1, ROWS + 128), f3...]
    unnamed x1 -> x0, blocking collectives: 58.2 us -> none
    all_to_all x2 -> x0, waiting for transfers between devices: 23 us -> none  [the longest x1 15.2 us: local(): lax.all_to_all(embeddings.reshape(blocks_total, per_peer, feature_dim), (...]
    all_to_all x2 -> x0, starting transfers between devices: 16.3 us -> none  [the longest x1 11.5 us: local(): lax.all_to_all(embeddings.reshape(blocks_total, per_peer, feature_dim), (...]
    all_gather x1 -> x0, blocking collectives: 9.64 us -> none  [local(): lax.all_gather(local_sign, 'row', axis=0, tiled=True)]
  transfers between devices with their start and end apart: 4 -> 0, of which waited for: 4 -> 0; matrix products, arithmetic and copies ran while one was open for 2% -> 0% of each run, Pallas kernels for 0% -> 0%
where the time goes in v2:
time: 78.6 us; the launch traced here: 78.4 us
  Pallas kernels  75.9 us (97%)
  local copies, waits for them, and re-layouts  1.81 us (2%)
    pallas_call x1, Pallas kernels, local(): pl.pallas_call(kernel, out_shape=jax.ShapeDtypeStruct((1, ROWS + 128), f3...  75.9 us
    slice x2, local copies, waits for them, and re-layouts, local(): return (result[0, :ROWS], result[0, ROWS])  1.81 us

profile of v2, /device:TPU:1, one launch (start us, length us, event | category | flops | bytes accessed | tf_op | source)
XLA Modules:
  0.0 78.4 jit_solution(4709692754993021558)
XLA Ops:
  0.6 75.9 %shard_map.50 = f32[1,384]{1,0:T(1,128)} custom-call(f32[256,768]{1,0:T(8,128)} %emb.1, s32[1,256]{1,0:T(1,128)} %bitcast.4, s32[1,256]{1,0:T(1,128)} %bitcast.5), custom_call_target="tpu_custom_call" | custom-call | tf_op jit(solution)/shard_map/pallas_call | solution.py:331
  76.6 0.0 copy-start
  76.6 1.2 %slice.7 = f32[1,1]{1,0:T(1,128)} slice(f32[1,384]{1,0:T(1,128)} %shard_map.50), slice={[0:1], [256:257]} | slice | bytes 8 | tf_op jit(solution)/shard_map/slice | solution.py:352
  77.8 0.0 copy-done
  77.8 0.6 slice.6
Async XLA Ops:
  76.6 1.3 %copy-start = (f32[1,384]{1,0:T(1,128)S(1)}, f32[1,384]{1,0:T(1,128)}, u32[]{:S(2)}) copy-start(f32[1,384]{1,0:T(1,128)} %shard_map.50) | copy-start | bytes 4612

commit v3 on v2

--- a/solution.py
+++ b/solution.py
@@ -18,8 +18,8 @@
 SCALE = math.sqrt(2.0 * math.log2(math.e) / 200.0)
 
 CHUNKS = 4
-ORDER = [(0, 0, 0), (0, 0, 1), (0, 0, 3), (0, 3, 0), (3, 0, 0), (0, 1, 3), (1, 3, 0), (0, 0, 2), (0, 1, 2), (1, 2, 0), (2, 0, 0), (2, 2, 0)]
-EDGES = [((0, 0, 0), (3, 0, 0)), ((0, 0, 0), (0, 0, 3)), ((0, 0, 0), (0, 3, 0)), ((0, 0, 0), (0, 0, 1)), ((0, 0, 3), (0, 1, 3)), ((0, 3, 0), (1, 3, 0)), ((3, 0, 0), (2, 0, 0)), ((0, 0, 1), (0, 0, 2)), ((0, 1, 3), (0, 1, 2)), ((1, 3, 0), (1, 2, 0)), ((1, 2, 0), (2, 2, 0))]
+ORDER = [(0, 0, 0), (0, 0, 1), (0, 0, 3), (0, 1, 0), (3, 0, 0), (1, 0, 3), (3, 3, 0), (0, 0, 2), (0, 2, 0), (1, 0, 2), (2, 3, 0), (2, 2, 0)]
+EDGES = [((0, 0, 0), (0, 1, 0)), ((0, 0, 0), (0, 0, 3)), ((0, 0, 0), (3, 0, 0)), ((0, 0, 0), (0, 0, 1)), ((0, 0, 1), (0, 0, 2)), ((0, 1, 0), (0, 2, 0)), ((0, 0, 3), (1, 0, 3)), ((3, 0, 0), (3, 3, 0)), ((1, 0, 3), (1, 0, 2)), ((3, 3, 0), (2, 3, 0)), ((2, 3, 0), (2, 2, 0))]
 PLAN = [
     ('fwd', 1, 0),
     ('fwd', 2, 0),
@@ -45,51 +45,37 @@
     ('share', 3),
     ('fwd', 4, 3),
     ('share', 4),
+    ('go', 1, (), (), (1,)),
     ('fwd', 5, 2),
+    ('go', 1, (0,), (), (2,)),
     ('fwd', 6, 2),
-    ('take', 1),
-    ('full', 1, (0,)),
-    ('take', 2),
-    ('half', 2, (1,)),
-    ('fwd', 9, 0),
-    ('take', 3),
-    ('full', 3, (0, 1)),
+    ('go', 2, (), (1,), (3,)),
+    ('fwd', 10, 0),
+    ('go', 3, (0, 1, 2), (), (4,)),
     ('fwd', 5, 3),
     ('share', 5),
+    ('go', 4, (0, 1, 2), (), ()),
     ('fwd', 6, 3),
     ('share', 6),
-    ('full', 3, (2,)),
-    ('take', 4),
-    ('full', 4, (0, 1)),
-    ('fwd', 9, 1),
-    ('full', 4, (2, 3)),
-    ('take', 5),
-    ('full', 5, (1, 3)),
-    ('fwd', 9, 2),
-    ('full', 5, (4,)),
-    ('take', 6),
-    ('full', 6, (1, 2, 4, 5)),
+    ('fwd', 10, 1),
+    ('go', 4, (3,), (), (5,)),
+    ('go', 5, (1, 3, 4), (), ()),
+    ('go', 6, (), (), (6,)),
+    ('fwd', 10, 2),
+    ('go', 6, (1, 2, 3, 5), (), ()),
     ('share', 7),
     ('share', 8),
-    ('fwd', 9, 3),
     ('share', 9),
+    ('fwd', 10, 3),
     ('share', 10),
-    ('take', 7),
-    ('full', 7, (4, 6)),
-    ('take', 8),
-    ('full', 8, (4, 6)),
-    ('half', 8, (3,)),
-    ('take', 9),
-    ('full', 9, (0, 1)),
+    ('go', 7, (), (), (7,)),
+    ('go', 7, (3, 6), (), (8,)),
+    ('go', 8, (1, 5, 6), (0, 7), (9,)),
+    ('go', 9, (3, 6, 8), (4,), (10,)),
     ('share', 11),
-    ('full', 9, (5,)),
-    ('half', 9, (4,)),
-    ('take', 10),
-    ('full', 10, (1, 5, 6, 8)),
-    ('half', 10, (0, 7)),
-    ('take', 11),
-    ('full', 11, (1, 5)),
-    ('half', 11, (7, 10)),
+    ('go', 10, (0, 1, 5), (3,), ()),
+    ('go', 11, (), (), (11,)),
+    ('go', 11, (1, 5), (7, 8), ()),
 ]
 
 DIRS = [(1, 0, 0), (3, 0, 0), (0, 1, 0), (0, 3, 0), (0, 0, 1), (0, 0, 3)]
@@ -98,12 +84,13 @@
 INDEX = {e: i for i, e in enumerate(ORDER)}
 STEP = ROWS // CHUNKS
 CHILDREN = {i: [INDEX[w] for u, w in EDGES if INDEX[u] == i] for i in range(COUNT)}
-PARENT = {INDEX[w]: INDEX[u] for u, w in EDGES}
 FIRST_SEM = {}
 SEMS = 0
 for _i in range(1, COUNT):
     FIRST_SEM[_i] = SEMS
     SEMS += CHUNKS if CHILDREN[_i] else 1
+STEPS = [p for p in PLAN if p[0] == "go"]
+LAST = {i: max([0] + [k for k, p in enumerate(STEPS) if (p[1] == i and p[2] + p[3]) or i in p[2] + p[3]]) for i in range(COUNT)}
 
 
 def minus(a, b):
@@ -125,9 +112,9 @@
 
 
 def kernel(
-    emb, lab, src, out,
-    raw, split, cols, row_acc, col_acc, part, part_in, stage, final,
-    load_sem, tree_send, tree_recv, sib_send, sib_recv, part_send, part_recv,
+    emb, lab_in, src_in, out,
+    lab, src, raw, split, cols, row_acc, col_acc, part, part_in, stage, final,
+    load_sem, lab_sem, src_sem, tree_send, tree_recv, sib_send, sib_recv, part_send, part_recv,
     row_send, row_recv, col_send, col_recv,
 ):
     row, col = lax.axis_index("row"), lax.axis_index("col")
@@ -150,6 +137,10 @@
 
     load = pltpu.make_async_copy(emb, raw.at[0, pl.ds(0, ROWS)], load_sem)
     load.start()
+    load_lab = pltpu.make_async_copy(lab_in, lab, lab_sem)
+    load_lab.start()
+    load_src = pltpu.make_async_copy(src_in, src, src_sem)
+    load_src.start()
     barrier = pltpu.get_barrier_semaphore()
     for offset in DIRS:
         pl.semaphore_signal(barrier, inc=1, device_id=device(offset), device_id_type=MESH)
@@ -159,6 +150,7 @@
     y = raw[0, pl.ds(0, ROWS)] * SCALE
     minus_half = -0.5 * jnp.sum(y * y, axis=1, keepdims=True)
     norm_row = jnp.transpose(jnp.broadcast_to(minus_half, (ROWS, 128)))[0:1]
+    load_lab.wait()
     sign_row = (1 - 2 * lab[...]).astype(jnp.float32)
     aux = jnp.concatenate([norm_row, sign_row, jnp.zeros((AUX - 2, ROWS), jnp.float32)], axis=0)
     raw[0, pl.ds(ROWS, AUX)] = jnp.concatenate([aux, jnp.zeros((AUX, D - ROWS), jnp.float32)], axis=1)
@@ -181,9 +173,8 @@
         return remote(raw.at[2 * i], raw.at[2 * i + 1], sib_send, sib_recv.at[i], other_core)
 
     def prepare(slot):
-        @pl.loop(0, ROWS // 64)
-        def _(t):
-            rows = pl.ds(pl.multiple_of(t * 64, 64), 64)
+        for start in range(0, ROWS, 32):
+            rows = pl.ds(start, 32)
             y = raw[slot, rows] * SCALE
             high = y.astype(jnp.bfloat16)
             split[slot, rows, :D] = high
@@ -204,30 +195,25 @@
             if both:
                 col_acc[slot] += jnp.sum((e * sign_i).reshape(ROWS // 8, 8, ROWS), axis=0)
 
-    def full(i, partners):
-        pairs = len(partners) // 2
-        if pairs > 1:
-            digits = sum(f << (4 * t) for t, f in enumerate(partners[:2 * pairs]))
-
-            @pl.loop(0, pairs)
-            def _(t):
-                both = lax.shift_right_logical(jnp.int32(digits), jnp.int32(8 * t))
-                b, c = both & 15, lax.shift_right_logical(both, jnp.int32(4)) & 15
-                work(i, [2 * b, 2 * b + 1, 2 * c, 2 * c + 1])
-        elif pairs:
-            b, c = partners[:2]
-            work(i, [2 * b, 2 * b + 1, 2 * c, 2 * c + 1])
-        if len(partners) % 2:
-            b = partners[-1]
-            work(i, [2 * b, 2 * b + 1])
-
-    def half(i, partners):
-        slots = []
-        for b in partners:
-            diff = minus(ORDER[i], ORDER[b])
-            axis = [t for t in range(3) if diff[t] == 2][0]
-            slots.append(2 * b + place[axis] // 2)
-        work(i, slots)
+    def half_slot(i, b):
+        diff = minus(ORDER[i], ORDER[b])
+        axis = [t for t in range(3) if diff[t] == 2][0]
+        return 2 * b + place[axis] // 2
+
+    def totals(i):
+        for slot in (2 * i, 2 * i + 1):
+            total = jnp.sum(col_acc[slot], axis=0, keepdims=True)
+            if slot % 2 == 0:
+                total = total + jnp.sum(jnp.transpose(row_acc[i]), axis=0, keepdims=True)
+            part[slot] = total
+
+    def send_totals(i):
+        for slot in (2 * i, 2 * i + 1):
+            if slot:
+                remote(
+                    part.at[slot], part_in.at[slot], part_send, part_recv,
+                    device(ORDER[i], slot % 2 == 1),
+                ).start()
 
     for chunk in range(CHUNKS):
         relay(0, chunk)
@@ -239,34 +225,36 @@
     prepare(1)
     work(0, [0, 1], False)
 
-    for op, i, *rest in PLAN:
-        if op == "fwd":
-            arrive(i, rest[0])
-            relay(i, rest[0])
-        elif op == "share":
-            if not CHILDREN[i]:
-                arrive(i, 0)
-            sibling(i).start()
-        elif op == "take":
-            prepare(2 * i)
-            sibling(i).wait_recv()
-            prepare(2 * i + 1)
-        elif op == "full":
-            full(i, rest[0])
-        else:
-            half(i, rest[0])
-
-    for slot in range(SLOTS):
-        i = slot // 2
-        total = jnp.sum(col_acc[slot], axis=0, keepdims=True)
-        if slot % 2 == 0:
-            total = total + jnp.sum(jnp.transpose(row_acc[i]), axis=0, keepdims=True)
-        part[slot] = total
-        if slot:
-            remote(
-                part.at[slot], part_in.at[slot], part_send, part_recv,
-                device(ORDER[i], slot % 2 == 1),
-            ).start()
+    step, sent = 0, set()
+    for op in PLAN:
+        if op[0] == "fwd":
+            arrive(op[1], op[2])
+            relay(op[1], op[2])
+            continue
+        if op[0] == "share":
+            if not CHILDREN[op[1]]:
+                arrive(op[1], 0)
+            sibling(op[1]).start()
+            continue
+        _, i, full, half, fresh = op
+        for w in fresh:
+            sibling(w).wait_recv()
+        done = [e for e in range(COUNT) if e not in sent and LAST[e] < step]
+        for e in done:
+            totals(e)
+        for w in fresh:
+            prepare(2 * w)
+            prepare(2 * w + 1)
+        work(i, [2 * b + t for b in full for t in range(CORES)] + [half_slot(i, b) for b in half])
+        for e in done:
+            send_totals(e)
+        sent.update(done)
+        step += 1
+    for e in range(COUNT):
+        if e not in sent:
+            totals(e)
+            send_totals(e)
+
     rest = pl.ds(1, SLOTS - 1)
     arrived = remote(part.at[rest], part_in.at[rest], part_send, part_recv, other_core)
     arrived.wait_recv()
@@ -305,6 +293,7 @@
     lane = lax.broadcasted_iota(jnp.int32, values.shape, 1)
     first = jnp.sum(jnp.where(lane == base + 2 * col, values, 0.0), axis=1, keepdims=True)
     second = jnp.sum(jnp.where(lane == base + 2 * col + 1, values, 0.0), axis=1, keepdims=True)
+    load_src.wait()
     ids = src[...]
     held = lax.broadcasted_iota(jnp.int32, (128, ROWS), 0)
     owner = (held % 8) * COLS_MESH + held // 8
@@ -331,9 +320,11 @@
     result = pl.pallas_call(
         kernel,
         out_shape=jax.ShapeDtypeStruct((1, ROWS + 128), f32),
-        in_specs=[pl.BlockSpec(memory_space=pl.ANY), vmem, vmem],
+        in_specs=[pl.BlockSpec(memory_space=pl.ANY)] * 3,
         out_specs=vmem,
         scratch_shapes=[
+            pltpu.VMEM((1, ROWS), jnp.int32),
+            pltpu.VMEM((1, ROWS), jnp.int32),
             pltpu.VMEM((SLOTS, ROWS + AUX, D), f32),
             pltpu.VMEM((SLOTS, ROWS, 2 * D), jnp.bfloat16),
             pltpu.VMEM((COUNT, ROWS, 128), f32),
@@ -343,7 +334,7 @@
             pltpu.VMEM((SLOTS, 1, ROWS), f32),
             pltpu.VMEM((ROWS_MESH, ROWS + 128), f32),
             pltpu.VMEM((ROWS_MESH * COLS_MESH, 128), f32),
-            dma, dma, dma((SEMS,)), dma, dma((COUNT,)), dma, dma, dma, dma, dma, dma,
+            dma, dma, dma, dma, dma((SEMS,)), dma, dma((COUNT,)), dma, dma, dma, dma, dma, dma,
         ],
         compiler_params=pltpu.CompilerParams(
             collective_id=0, has_side_effects=True, vmem_limit_bytes=56 * 2**20

time: 78.6 us -> 75.3 us (0.958)
  Pallas kernels: 75.9 us -> 72.7 us
    pallas_call x1, Pallas kernels: 75.9 us -> 72.7 us  [local(): pl.pallas_call(kernel, out_shape=jax.ShapeDtypeStruct((1, ROWS + 128), f3...]
where the time goes in v3:
time: 75.3 us; the launch traced here: 75.2 us
  Pallas kernels  72.7 us (97%)
  local copies, waits for them, and re-layouts  1.81 us (2%)
    pallas_call x1, Pallas kernels, local(): pl.pallas_call(kernel, out_shape=jax.ShapeDtypeStruct((1, ROWS + 128), f3...  72.7 us
    slice x2, local copies, waits for them, and re-layouts, local(): return (result[0, :ROWS], result[0, ROWS])  1.81 us

profile of v3, /device:TPU:1, one launch (start us, length us, event | category | flops | bytes accessed | tf_op | source)
XLA Modules:
  0.0 75.2 jit_solution(17355337215086205482)
XLA Ops:
  0.6 72.7 %shard_map.50 = f32[1,384]{1,0:T(1,128)} custom-call(f32[256,768]{1,0:T(8,128)} %emb.1, s32[1,256]{1,0:T(1,128)} %bitcast.4, s32[1,256]{1,0:T(1,128)} %bitcast.5), custom_call_target="tpu_custom_call" | custom-call | tf_op jit(solution)/shard_map/pallas_call | solution.py:320
  73.4 0.0 copy-start
  73.4 1.2 %slice.7 = f32[1,1]{1,0:T(1,128)} slice(f32[1,384]{1,0:T(1,128)} %shard_map.50), slice={[0:1], [256:257]} | slice | bytes 8 | tf_op jit(solution)/shard_map/slice | solution.py:343
  74.6 0.0 copy-done
  74.6 0.6 slice.6
Async XLA Ops:
  73.4 1.3 %copy-start = (f32[1,384]{1,0:T(1,128)S(1)}, f32[1,384]{1,0:T(1,128)}, u32[]{:S(2)}) copy-start(f32[1,384]{1,0:T(1,128)} %shard_map.50) | copy-start | bytes 4612

commit v4 on v3

--- a/solution.py
+++ b/solution.py
@@ -17,7 +17,7 @@
 HALF_COUNT = 16384
 SCALE = math.sqrt(2.0 * math.log2(math.e) / 200.0)
 
-CHUNKS = 4
+SIZES = (32, 48, 56, 56, 64)
 ORDER = [(0, 0, 0), (0, 0, 1), (0, 0, 3), (0, 1, 0), (3, 0, 0), (1, 0, 3), (3, 3, 0), (0, 0, 2), (0, 2, 0), (1, 0, 2), (2, 3, 0), (2, 2, 0)]
 EDGES = [((0, 0, 0), (0, 1, 0)), ((0, 0, 0), (0, 0, 3)), ((0, 0, 0), (3, 0, 0)), ((0, 0, 0), (0, 0, 1)), ((0, 0, 1), (0, 0, 2)), ((0, 1, 0), (0, 2, 0)), ((0, 0, 3), (1, 0, 3)), ((3, 0, 0), (3, 3, 0)), ((1, 0, 3), (1, 0, 2)), ((3, 3, 0), (2, 3, 0)), ((2, 3, 0), (2, 2, 0))]
 PLAN = [
@@ -38,51 +38,59 @@
     ('fwd', 5, 1),
     ('fwd', 6, 1),
     ('fwd', 1, 3),
+    ('fwd', 2, 3),
+    ('fwd', 3, 3),
+    ('fwd', 4, 3),
+    ('fwd', 5, 2),
+    ('fwd', 6, 2),
+    ('fwd', 1, 4),
     ('share', 1),
-    ('fwd', 2, 3),
+    ('fwd', 2, 4),
     ('share', 2),
-    ('fwd', 3, 3),
+    ('fwd', 3, 4),
     ('share', 3),
-    ('fwd', 4, 3),
+    ('fwd', 4, 4),
     ('share', 4),
-    ('go', 1, (), (), (1,)),
-    ('fwd', 5, 2),
-    ('go', 1, (0,), (), (2,)),
-    ('fwd', 6, 2),
-    ('go', 2, (), (1,), (3,)),
+    ('go', 1, (), (), (1,), ()),
+    ('go', 1, (0,), (), (2,), ()),
+    ('fwd', 5, 3),
     ('fwd', 10, 0),
-    ('go', 3, (0, 1, 2), (), (4,)),
-    ('fwd', 5, 3),
+    ('fwd', 6, 3),
+    ('go', 3, (), (), (3,), (1,)),
+    ('go', 2, (), (1,), (4,), (2,)),
+    ('go', 3, (0, 1, 2), (), (), (3,)),
+    ('fwd', 10, 1),
+    ('go', 4, (0, 1, 2), (), (), (4,)),
+    ('fwd', 5, 4),
     ('share', 5),
-    ('go', 4, (0, 1, 2), (), ()),
-    ('fwd', 6, 3),
+    ('fwd', 6, 4),
     ('share', 6),
-    ('fwd', 10, 1),
-    ('go', 4, (3,), (), (5,)),
-    ('go', 5, (1, 3, 4), (), ()),
-    ('go', 6, (), (), (6,)),
+    ('go', 4, (3,), (), (5,), ()),
     ('fwd', 10, 2),
-    ('go', 6, (1, 2, 3, 5), (), ()),
+    ('go', 5, (1, 3, 4), (), (6,), ()),
+    ('go', 6, (1, 2, 3), (), (), (5,)),
+    ('fwd', 10, 3),
+    ('go', 6, (5,), (), (), (6,)),
     ('share', 7),
     ('share', 8),
     ('share', 9),
-    ('fwd', 10, 3),
+    ('fwd', 10, 4),
     ('share', 10),
-    ('go', 7, (), (), (7,)),
-    ('go', 7, (3, 6), (), (8,)),
-    ('go', 8, (1, 5, 6), (0, 7), (9,)),
-    ('go', 9, (3, 6, 8), (4,), (10,)),
+    ('go', 7, (), (), (7,), ()),
+    ('go', 7, (3, 6), (), (8,), ()),
+    ('go', 8, (1, 5, 6), (0,), (9,), (7,)),
+    ('go', 8, (), (7,), (10,), (8,)),
+    ('go', 9, (3, 6, 8), (4,), (), ()),
     ('share', 11),
-    ('go', 10, (0, 1, 5), (3,), ()),
-    ('go', 11, (), (), (11,)),
-    ('go', 11, (1, 5), (7, 8), ()),
+    ('go', 10, (0, 1, 5), (3,), (11,), ()),
+    ('go', 11, (1, 5), (7, 8), (), ()),
 ]
 
 DIRS = [(1, 0, 0), (3, 0, 0), (0, 1, 0), (0, 3, 0), (0, 0, 1), (0, 0, 3)]
 COUNT = len(ORDER)
 SLOTS = CORES * COUNT
 INDEX = {e: i for i, e in enumerate(ORDER)}
-STEP = ROWS // CHUNKS
+CHUNKS = len(SIZES)
 CHILDREN = {i: [INDEX[w] for u, w in EDGES if INDEX[u] == i] for i in range(COUNT)}
 FIRST_SEM = {}
 SEMS = 0
@@ -90,6 +98,7 @@
     FIRST_SEM[_i] = SEMS
     SEMS += CHUNKS if CHILDREN[_i] else 1
 STEPS = [p for p in PLAN if p[0] == "go"]
+SHARED = {0} | {b for p in STEPS for b in p[2] + p[3]}
 LAST = {i: max([0] + [k for k, p in enumerate(STEPS) if (p[1] == i and p[2] + p[3]) or i in p[2] + p[3]]) for i in range(COUNT)}
 
 
@@ -98,8 +107,7 @@
 
 
 def span(chunk):
-    start = chunk * STEP
-    return pl.ds(start, STEP + (AUX if chunk == CHUNKS - 1 else 0))
+    return pl.ds(sum(SIZES[:chunk]), SIZES[chunk] + (AUX if chunk == CHUNKS - 1 else 0))
 
 
 def product(a, b):
@@ -208,12 +216,11 @@
             part[slot] = total
 
     def send_totals(i):
-        for slot in (2 * i, 2 * i + 1):
-            if slot:
-                remote(
-                    part.at[slot], part_in.at[slot], part_send, part_recv,
-                    device(ORDER[i], slot % 2 == 1),
-                ).start()
+        if i:
+            rows = pl.ds(2 * i, 2)
+            remote(
+                part.at[rows], part_in.at[rows], part_send, part_recv, device(ORDER[i])
+            ).start()
 
     for chunk in range(CHUNKS):
         relay(0, chunk)
@@ -234,16 +241,18 @@
         if op[0] == "share":
             if not CHILDREN[op[1]]:
                 arrive(op[1], 0)
-            sibling(op[1]).start()
+            if op[1] in SHARED:
+                sibling(op[1]).start()
             continue
-        _, i, full, half, fresh = op
-        for w in fresh:
+        _, i, full, half, own, other = op
+        for w in other:
             sibling(w).wait_recv()
         done = [e for e in range(COUNT) if e not in sent and LAST[e] < step]
         for e in done:
             totals(e)
-        for w in fresh:
+        for w in own:
             prepare(2 * w)
+        for w in other:
             prepare(2 * w + 1)
         work(i, [2 * b + t for b in full for t in range(CORES)] + [half_slot(i, b) for b in half])
         for e in done:
@@ -255,27 +264,31 @@
             totals(e)
             send_totals(e)
 
-    rest = pl.ds(1, SLOTS - 1)
+    rest = pl.ds(2, SLOTS - 2)
     arrived = remote(part.at[rest], part_in.at[rest], part_send, part_recv, other_core)
     arrived.wait_recv()
-    proof = part[0]
-    for slot in range(1, SLOTS):
-        proof = proof + part_in[slot]
-    proof = proof * (1000.0 / HALF_COUNT)
-    here = jnp.sum(proof * sign_row, axis=1, keepdims=True)
-    stage[pl.ds(row, 1), :] = jnp.concatenate([proof, jnp.broadcast_to(here, (1, 128))], axis=1)
+    mine, his = part[0], part[1]
+    for i in range(1, COUNT):
+        mine, his = mine + part_in[2 * i], his + part_in[2 * i + 1]
+    mine, his = mine * (1000.0 / HALF_COUNT), his * (1000.0 / HALF_COUNT)
+    his_sign = raw[1, pl.ds(ROWS, AUX), :ROWS][1:2]
+    here = jnp.sum(mine * sign_row + his * his_sign, axis=1, keepdims=True)
+    zero, one = jnp.where(core == 0, mine, his), jnp.where(core == 0, his, mine)
+    tail = jnp.broadcast_to(here, (1, 128))
+    stage[row] = jnp.concatenate(
+        [jnp.concatenate([zero, tail], axis=1), jnp.concatenate([one, tail], axis=1)], axis=0
+    )
 
     for k in range(1, ROWS_MESH):
-        mine = stage.at[pl.ds(row, 1)]
-        remote(mine, mine, row_send, row_recv, ((row + k) % ROWS_MESH, col)).start()
-    seven = remote(
-        raw.at[0, pl.ds(0, ROWS_MESH - 1), pl.ds(0, ROWS + 128)],
-        raw.at[0, pl.ds(0, ROWS_MESH - 1), pl.ds(0, ROWS + 128)],
-        row_send, row_recv, other_core,
-    )
+        block = stage.at[row]
+        remote(block, block, row_send, row_recv, ((row + k) % ROWS_MESH, col)).start()
+    others = stage.at[pl.ds(1, ROWS_MESH - 1)]
+    seven = remote(others, others, row_send, row_recv, other_core)
     seven.wait_recv()
-    window = jnp.where(row < ROWS_MESH // 2, stage[:, :128], stage[:, 128:256])
-    column_total = jnp.sum(stage[:, 256:], axis=0, keepdims=True)
+    halves = [stage[2 * z] + stage[2 * z + 1] for z in range(ROWS_MESH // 2)]
+    sums = jnp.concatenate(halves, axis=0)
+    window = jnp.where(row < ROWS_MESH // 2, sums[:, :128], sums[:, 128:256])
+    column_total = 0.5 * jnp.sum(sums[:, 256:], axis=0, keepdims=True)
     lane = lax.broadcasted_iota(jnp.int32, (8, 128), 1)
     base = (row % 4) * 32
     window = jnp.where((lane >= base) & (lane < base + 32), window, column_total)
@@ -306,7 +319,7 @@
 
     tree = raw.at[pl.ds(0, COUNT - 1)]
     remote(tree, tree, tree_send, load_sem, other_core).wait_send()
-    shared = raw.at[pl.ds(0, COUNT)]
+    shared = raw.at[pl.ds(0, len(SHARED))]
     remote(shared, shared, sib_send, load_sem, other_core).wait_send()
     arrived.wait_send()
     seven.wait_send()
@@ -332,7 +345,7 @@
             pltpu.VMEM((SLOTS, 8, ROWS), f32),
             pltpu.VMEM((SLOTS, 1, ROWS), f32),
             pltpu.VMEM((SLOTS, 1, ROWS), f32),
-            pltpu.VMEM((ROWS_MESH, ROWS + 128), f32),
+            pltpu.VMEM((ROWS_MESH, 2, ROWS + 128), f32),
             pltpu.VMEM((ROWS_MESH * COLS_MESH, 128), f32),
             dma, dma, dma, dma, dma((SEMS,)), dma, dma((COUNT,)), dma, dma, dma, dma, dma, dma,
         ],

time: 75.3 us -> 73.7 us (0.979)
  Pallas kernels: 72.7 us -> 71.1 us
    pallas_call x1, Pallas kernels: 72.7 us -> 71.1 us  [local(): pl.pallas_call(kernel, out_shape=jax.ShapeDtypeStruct((1, ROWS + 128), f3...]
where the time goes in v4:
time: 73.7 us; the launch traced here: 73.6 us
  Pallas kernels  71.1 us (96%)
  local copies, waits for them, and re-layouts  1.81 us (2%)
    pallas_call x1, Pallas kernels, local(): pl.pallas_call(kernel, out_shape=jax.ShapeDtypeStruct((1, ROWS + 128), f3...  71.1 us
    slice x2, local copies, waits for them, and re-layouts, local(): return (result[0, :ROWS], result[0, ROWS])  1.81 us

profile of v4, /device:TPU:1, one launch (start us, length us, event | category | flops | bytes accessed | tf_op | source)
XLA Modules:
  0.0 73.6 jit_solution(9846723282881411860)
XLA Ops:
  0.6 71.1 %shard_map.50 = f32[1,384]{1,0:T(1,128)} custom-call(f32[256,768]{1,0:T(8,128)} %emb.1, s32[1,256]{1,0:T(1,128)} %bitcast.4, s32[1,256]{1,0:T(1,128)} %bitcast.5), custom_call_target="tpu_custom_call" | custom-call | tf_op jit(solution)/shard_map/pallas_call | solution.py:333
  71.7 0.0 copy-start
  71.7 1.2 %slice.7 = f32[1,1]{1,0:T(1,128)} slice(f32[1,384]{1,0:T(1,128)} %shard_map.50), slice={[0:1], [256:257]} | slice | bytes 8 | tf_op jit(solution)/shard_map/slice | solution.py:356
  73.0 0.0 copy-done
  73.0 0.6 slice.6
Async XLA Ops:
  71.7 1.3 %copy-start = (f32[1,384]{1,0:T(1,128)S(1)}, f32[1,384]{1,0:T(1,128)}, u32[]{:S(2)}) copy-start(f32[1,384]{1,0:T(1,128)} %shard_map.50) | copy-start | bytes 4612

commit v5 on v4

--- a/solution.py
+++ b/solution.py
@@ -18,8 +18,8 @@
 SCALE = math.sqrt(2.0 * math.log2(math.e) / 200.0)
 
 SIZES = (32, 48, 56, 56, 64)
-ORDER = [(0, 0, 0), (0, 0, 1), (0, 0, 3), (0, 1, 0), (3, 0, 0), (1, 0, 3), (3, 3, 0), (0, 0, 2), (0, 2, 0), (1, 0, 2), (2, 3, 0), (2, 2, 0)]
-EDGES = [((0, 0, 0), (0, 1, 0)), ((0, 0, 0), (0, 0, 3)), ((0, 0, 0), (3, 0, 0)), ((0, 0, 0), (0, 0, 1)), ((0, 0, 1), (0, 0, 2)), ((0, 1, 0), (0, 2, 0)), ((0, 0, 3), (1, 0, 3)), ((3, 0, 0), (3, 3, 0)), ((1, 0, 3), (1, 0, 2)), ((3, 3, 0), (2, 3, 0)), ((2, 3, 0), (2, 2, 0))]
+ORDER = [(0, 0, 0), (0, 0, 1), (0, 0, 3), (0, 3, 0), (3, 0, 0), (0, 1, 3), (1, 3, 0), (0, 0, 2), (0, 1, 2), (1, 2, 0), (2, 0, 0), (2, 2, 0)]
+EDGES = [((0, 0, 0), (3, 0, 0)), ((0, 0, 0), (0, 0, 3)), ((0, 0, 0), (0, 3, 0)), ((0, 0, 0), (0, 0, 1)), ((0, 0, 3), (0, 1, 3)), ((0, 3, 0), (1, 3, 0)), ((3, 0, 0), (2, 0, 0)), ((0, 0, 1), (0, 0, 2)), ((0, 1, 3), (0, 1, 2)), ((1, 3, 0), (1, 2, 0)), ((1, 2, 0), (2, 2, 0))]
 PLAN = [
     ('fwd', 1, 0),
     ('fwd', 2, 0),
@@ -54,36 +54,36 @@
     ('go', 1, (), (), (1,), ()),
     ('go', 1, (0,), (), (2,), ()),
     ('fwd', 5, 3),
-    ('fwd', 10, 0),
     ('fwd', 6, 3),
+    ('fwd', 9, 0),
     ('go', 3, (), (), (3,), (1,)),
     ('go', 2, (), (1,), (4,), (2,)),
     ('go', 3, (0, 1, 2), (), (), (3,)),
-    ('fwd', 10, 1),
+    ('fwd', 9, 1),
     ('go', 4, (0, 1, 2), (), (), (4,)),
     ('fwd', 5, 4),
     ('share', 5),
     ('fwd', 6, 4),
     ('share', 6),
     ('go', 4, (3,), (), (5,), ()),
-    ('fwd', 10, 2),
+    ('fwd', 9, 2),
     ('go', 5, (1, 3, 4), (), (6,), ()),
-    ('go', 6, (1, 2, 3), (), (), (5,)),
-    ('fwd', 10, 3),
+    ('go', 6, (1, 2, 4), (), (), (5,)),
+    ('fwd', 9, 3),
     ('go', 6, (5,), (), (), (6,)),
     ('share', 7),
     ('share', 8),
+    ('fwd', 9, 4),
     ('share', 9),
-    ('fwd', 10, 4),
     ('share', 10),
     ('go', 7, (), (), (7,), ()),
-    ('go', 7, (3, 6), (), (8,), ()),
-    ('go', 8, (1, 5, 6), (0,), (9,), (7,)),
-    ('go', 8, (), (7,), (10,), (8,)),
-    ('go', 9, (3, 6, 8), (4,), (), ()),
+    ('go', 7, (4, 6), (), (8,), ()),
+    ('go', 8, (4, 6), (3,), (9,), (7,)),
+    ('go', 9, (0, 1, 5), (4,), (10,), (8,)),
+    ('go', 10, (1, 5, 6, 8), (0, 7), (), (10,)),
     ('share', 11),
-    ('go', 10, (0, 1, 5), (3,), (11,), ()),
-    ('go', 11, (1, 5), (7, 8), (), ()),
+    ('go', 11, (), (), (11,), ()),
+    ('go', 11, (1, 5), (7, 10), (), ()),
 ]
 
 DIRS = [(1, 0, 0), (3, 0, 0), (0, 1, 0), (0, 3, 0), (0, 0, 1), (0, 0, 3)]

time: 73.7 us -> 73.1 us (level)
  no operation moved by 1% of the time
where the time goes in v5:
time: 73.1 us; the launch traced here: 72.9 us
  Pallas kernels  70.5 us (96%)
  local copies, waits for them, and re-layouts  1.81 us (2%)
    pallas_call x1, Pallas kernels, local(): pl.pallas_call(kernel, out_shape=jax.ShapeDtypeStruct((1, ROWS + 128), f3...  70.5 us
    slice x2, local copies, waits for them, and re-layouts, local(): return (result[0, :ROWS], result[0, ROWS])  1.81 us

profile of v5, /device:TPU:1, one launch (start us, length us, event | category | flops | bytes accessed | tf_op | source)
XLA Modules:
  0.0 72.9 jit_solution(3999964786528579211)
XLA Ops:
  0.6 70.5 %shard_map.50 = f32[1,384]{1,0:T(1,128)} custom-call(f32[256,768]{1,0:T(8,128)} %emb.1, s32[1,256]{1,0:T(1,128)} %bitcast.4, s32[1,256]{1,0:T(1,128)} %bitcast.5), custom_call_target="tpu_custom_call" | custom-call | tf_op jit(solution)/shard_map/pallas_call | solution.py:333
  71.1 0.0 copy-start
  71.1 1.2 %slice.7 = f32[1,1]{1,0:T(1,128)} slice(f32[1,384]{1,0:T(1,128)} %shard_map.50), slice={[0:1], [256:257]} | slice | bytes 8 | tf_op jit(solution)/shard_map/slice | solution.py:356
  72.4 0.0 copy-done
  72.4 0.6 slice.6
Async XLA Ops:
  71.1 1.3 %copy-start = (f32[1,384]{1,0:T(1,128)S(1)}, f32[1,384]{1,0:T(1,128)}, u32[]{:S(2)}) copy-start(f32[1,384]{1,0:T(1,128)} %shard_map.50) | copy-start | bytes 4612

commit v6 on v5

--- a/solution.py
+++ b/solution.py
@@ -17,7 +17,7 @@
 HALF_COUNT = 16384
 SCALE = math.sqrt(2.0 * math.log2(math.e) / 200.0)
 
-SIZES = (32, 48, 56, 56, 64)
+SIZES = (40, 56, 56, 56, 48)
 ORDER = [(0, 0, 0), (0, 0, 1), (0, 0, 3), (0, 3, 0), (3, 0, 0), (0, 1, 3), (1, 3, 0), (0, 0, 2), (0, 1, 2), (1, 2, 0), (2, 0, 0), (2, 2, 0)]
 EDGES = [((0, 0, 0), (3, 0, 0)), ((0, 0, 0), (0, 0, 3)), ((0, 0, 0), (0, 3, 0)), ((0, 0, 0), (0, 0, 1)), ((0, 0, 3), (0, 1, 3)), ((0, 3, 0), (1, 3, 0)), ((3, 0, 0), (2, 0, 0)), ((0, 0, 1), (0, 0, 2)), ((0, 1, 3), (0, 1, 2)), ((1, 3, 0), (1, 2, 0)), ((1, 2, 0), (2, 2, 0))]
 PLAN = [
@@ -53,24 +53,24 @@
     ('share', 4),
     ('go', 1, (), (), (1,), ()),
     ('go', 1, (0,), (), (2,), ()),
+    ('go', 3, (), (), (3,), (1,)),
+    ('fwd', 9, 0),
+    ('go', 2, (), (1,), (4,), (2,)),
     ('fwd', 5, 3),
     ('fwd', 6, 3),
-    ('fwd', 9, 0),
-    ('go', 3, (), (), (3,), (1,)),
-    ('go', 2, (), (1,), (4,), (2,)),
     ('go', 3, (0, 1, 2), (), (), (3,)),
-    ('fwd', 9, 1),
     ('go', 4, (0, 1, 2), (), (), (4,)),
     ('fwd', 5, 4),
     ('share', 5),
     ('fwd', 6, 4),
     ('share', 6),
+    ('fwd', 9, 1),
     ('go', 4, (3,), (), (5,), ()),
+    ('go', 5, (1, 3, 4), (), (6,), ()),
     ('fwd', 9, 2),
-    ('go', 5, (1, 3, 4), (), (6,), ()),
     ('go', 6, (1, 2, 4), (), (), (5,)),
+    ('go', 6, (5,), (), (), (6,)),
     ('fwd', 9, 3),
-    ('go', 6, (5,), (), (), (6,)),
     ('share', 7),
     ('share', 8),
     ('fwd', 9, 4),

time: 73.1 us -> 73.1 us (level)
  no operation moved by 1% of the time
where the time goes in v6:
time: 73.1 us; the launch traced here: 73 us
  Pallas kernels  70.5 us (96%)
  local copies, waits for them, and re-layouts  1.81 us (2%)
    pallas_call x1, Pallas kernels, local(): pl.pallas_call(kernel, out_shape=jax.ShapeDtypeStruct((1, ROWS + 128), f3...  70.5 us
    slice x2, local copies, waits for them, and re-layouts, local(): return (result[0, :ROWS], result[0, ROWS])  1.81 us

profile of v6, /device:TPU:1, one launch (start us, length us, event | category | flops | bytes accessed | tf_op | source)
XLA Modules:
  0.0 73.0 jit_solution(5441886098985525265)
XLA Ops:
  0.6 70.5 %shard_map.50 = f32[1,384]{1,0:T(1,128)} custom-call(f32[256,768]{1,0:T(8,128)} %emb.1, s32[1,256]{1,0:T(1,128)} %bitcast.4, s32[1,256]{1,0:T(1,128)} %bitcast.5), custom_call_target="tpu_custom_call" | custom-call | tf_op jit(solution)/shard_map/pallas_call | solution.py:333
  71.1 0.0 copy-start
  71.1 1.2 %slice.7 = f32[1,1]{1,0:T(1,128)} slice(f32[1,384]{1,0:T(1,128)} %shard_map.50), slice={[0:1], [256:257]} | slice | bytes 8 | tf_op jit(solution)/shard_map/slice | solution.py:356
  72.4 0.0 copy-done
  72.4 0.6 slice.6
Async XLA Ops:
  71.1 1.3 %copy-start = (f32[1,384]{1,0:T(1,128)S(1)}, f32[1,384]{1,0:T(1,128)}, u32[]{:S(2)}) copy-start(f32[1,384]{1,0:T(1,128)} %shard_map.50) | copy-start | bytes 4612
